TPU v7x, 32 devices: a whole 2x2x4 slice. The times are simulated.
32 devices in a mesh: gx: 8 (over z, core), gy: 4 (over y, x).
Axes of the slice: x: 2, y: 2, z: 4, core: 2. Of those that a mesh axis runs over, the one named last changes fastest.
Arguments:
- net_inputs: bfloat16 [25, 1572864], P(None, ('gx', 'gy')), may hold values from -6 to 6
- velocity: float32 [3, 1572864], P(None, ('gx', 'gy'))
- particle_mass: float32 [1572864], P(('gx', 'gy')), may hold values from 0.5 to 2
- block_column: int32 [12288], P(('gx', 'gy')), may hold values from 0 to 8191, as said below
- cell_height: int32 [1572864], P(('gx', 'gy')), may hold values from 0 to 127
- block_counts: int32 [32], replicated, may hold values from 48 to 384, as said below
- cotangent: float32 [3, 1572864], P(None, ('gx', 'gy'))
- input_weight: bfloat16 [80, 25], replicated, may hold values from -1.25 to 1.25
- input_bias: float32 [80], replicated, may hold values from -3 to 3
- middle_weight: bfloat16 [80, 80], replicated, may hold values from -0.625 to 0.625
- middle_bias: float32 [80], replicated, may hold values from -3 to 3
- output_weight: bfloat16 [9, 80], replicated, may hold values from -0.625 to 0.625
- output_bias: float32 [9], replicated, may hold values from -3 to 3
Outputs:
- new_velocity: float32 [3, 1572864], P(None, ('gx', 'gy'))
- input_weight_grad: float32 [80, 25], replicated
- input_bias_grad: float32 [80], replicated
- middle_weight_grad: float32 [80, 80], replicated
- middle_bias_grad: float32 [80], replicated
- output_weight_grad: float32 [9, 80], replicated
- output_bias_grad: float32 [9], replicated
Inputs may be any that keep to these rules, and one draw needn't show every extreme that they name: `block_column`: the column of a block is 64 X + Y. Every block stored on the device at mesh position (i, j), i along gx, has X within i * 16 - 1 to i * 16 + 16 and Y within j * 16 - 1 to j * 16 + 16, both taken periodically over 128 and 64. `block_counts`: entry i * 4 + j counts the live blocks of the device at mesh position (i, j); they fill that device's first slots. One device, drawn from the seed, has all 384 live.
All inputs are finite; a program needn't handle non-finite values.
Results may differ from a plain program's by a relative error of at most 0.0056.
Values sent between devices are 32-bit elements; how exact they have to be, the bound alone decides.
A program may use at most 64 MiB of HBM per device.

v0:
```python
import jax
import jax.numpy as jnp
from jax import lax
from jax.sharding import PartitionSpec as P

CX = 16
CY = 16
NZ = 128
PB = 384
BLOCK = 128
GROUP = 64


time_scale = 0.5
epsilon = 1e-06


def with_halo(x, sides, width):
    for axis, dim in sides:
        size, length = (lax.axis_size(axis), x.shape[dim])
        up = [(i, (i + 1) % size) for i in range(size)]
        down = [(j, i) for i, j in up]
        last = lax.slice_in_dim(x, length - width, length, axis=dim)
        initial = lax.slice_in_dim(x, 0, width, axis=dim)
        before = lax.ppermute(last, axis, up)
        after = lax.ppermute(initial, axis, down)
        x = jnp.concatenate([before, x, after], axis=dim)
    return x


def network(
    inputs, input_weight, input_bias, middle_weight, middle_bias, output_weight, output_bias
):
    first = jnp.dot(input_weight, inputs, preferred_element_type=jnp.float32) + input_bias[:, None]
    first_act = jax.nn.silu(first).astype(jnp.bfloat16)
    second = (
        jnp.dot(middle_weight, first_act, preferred_element_type=jnp.float32) + middle_bias[:, None]
    )
    second_act = jax.nn.silu(second).astype(jnp.bfloat16)
    stress = (
        jnp.dot(output_weight, second_act, preferred_element_type=jnp.float32)
        + output_bias[:, None]
    )
    return (first, first_act, second, second_act, stress)


def silu_slope(values):
    sigmoid = jax.nn.sigmoid(values)
    return sigmoid * (1.0 + values * (1.0 - sigmoid))


def network_grads(
    inputs,
    stress_cot,
    input_weight,
    input_bias,
    middle_weight,
    middle_bias,
    output_weight,
    output_bias,
):
    first, first_act, second, second_act, stress = network(
        inputs, input_weight, input_bias, middle_weight, middle_bias, output_weight, output_bias
    )
    stress_cot_low = stress_cot.astype(jnp.bfloat16)
    output_weight_grad = jnp.dot(stress_cot_low, second_act.T, preferred_element_type=jnp.float32)
    output_bias_grad = jnp.sum(stress_cot, axis=1)
    second_cot = jnp.dot(
        output_weight.T, stress_cot_low, preferred_element_type=jnp.float32
    ) * silu_slope(second)
    second_low = second_cot.astype(jnp.bfloat16)
    middle_weight_grad = jnp.dot(second_low, first_act.T, preferred_element_type=jnp.float32)
    middle_bias_grad = jnp.sum(second_cot, axis=1)
    first_cot = jnp.dot(
        middle_weight.T, second_low, preferred_element_type=jnp.float32
    ) * silu_slope(first)
    first_low = first_cot.astype(jnp.bfloat16)
    input_weight_grad = jnp.dot(first_low, inputs.T, preferred_element_type=jnp.float32)
    input_bias_grad = jnp.sum(first_cot, axis=1)
    return (
        input_weight_grad,
        input_bias_grad,
        middle_weight_grad,
        middle_bias_grad,
        output_weight_grad,
        output_bias_grad,
    )


def vertical(field):
    widths = [(0, 0)] * (field.ndim - 1) + [(1, 1)]
    padded = jnp.pad(field, widths)
    return 0.5 * (padded[..., 2:] - padded[..., :-2])


def divergence(padded):
    shaped = padded.reshape((3, 3) + padded.shape[1:])
    along_x = 0.5 * (shaped[:, 0, 2:, 1:-1] - shaped[:, 0, :-2, 1:-1])
    along_y = 0.5 * (shaped[:, 1, 1:-1, 2:] - shaped[:, 1, 1:-1, :-2])
    return along_x + along_y + vertical(shaped[:, 2, 1:-1, 1:-1])


def stress_adjoint(padded):
    along_x = 0.5 * (padded[:, :-2, 1:-1] - padded[:, 2:, 1:-1])
    along_y = 0.5 * (padded[:, 1:-1, :-2] - padded[:, 1:-1, 2:])
    along_z = -vertical(padded[:, 1:-1, 1:-1])
    stacked = jnp.stack([along_x, along_y, along_z], axis=1)
    return stacked.reshape((9,) + along_x.shape[1:])


def height_selector(cell_height, start):
    heights = lax.dynamic_slice_in_dim(cell_height, start * BLOCK, GROUP * BLOCK, 0).reshape(
        GROUP, BLOCK
    )
    return (heights[:, :, None] == jnp.arange(NZ, dtype=jnp.int32)[None, None, :]).astype(
        jnp.float32
    )


def fold_deposit(values, cell_height, block_ext):
    channels = values.shape[0]

    def group_sums(group_index):
        start = group_index * GROUP
        piece_values = lax.dynamic_slice_in_dim(values, start * BLOCK, GROUP * BLOCK, 1).reshape(
            channels, GROUP, BLOCK
        )
        selector = height_selector(cell_height, start)
        return jnp.einsum("cbp,bpz->bcz", piece_values, selector, precision=lax.Precision.HIGHEST)

    per_block = lax.map(group_sums, jnp.arange(PB // GROUP, dtype=jnp.int32)).reshape(
        PB, channels, NZ
    )
    cell_sums = (
        jnp.zeros(((CX + 2) * (CY + 2), channels, NZ), jnp.float32).at[block_ext].add(per_block)
    )
    cell_sums = cell_sums.reshape(CX + 2, CY + 2, channels, NZ).transpose(2, 0, 1, 3)
    padded = with_halo(cell_sums, (("gx", 1), ("gy", 2)), 1)
    folded = padded[:, 2 : CX + 2]
    folded = folded.at[:, 0].add(padded[:, 0]).at[:, CX - 1].add(padded[:, CX + 3])
    result = folded[:, :, 2 : CY + 2]
    return result.at[:, :, 0].add(folded[:, :, 0]).at[:, :, CY - 1].add(folded[:, :, CY + 3])


def read_cells(grid_ext, cell_height, block_ext):
    channels = grid_ext.shape[0]
    flat_grid = grid_ext.reshape(channels, -1, NZ)

    def group_read(group_index):
        start = group_index * GROUP
        columns = lax.dynamic_slice_in_dim(block_ext, start, GROUP, 0)
        column_rows = flat_grid[:, columns]
        selector = height_selector(cell_height, start)
        picked = jnp.einsum("cbz,bpz->cbp", column_rows, selector, precision=lax.Precision.HIGHEST)
        return picked.reshape(channels, GROUP * BLOCK)

    stacked = lax.map(group_read, jnp.arange(PB // GROUP, dtype=jnp.int32))
    return stacked.transpose(1, 0, 2).reshape(channels, PB * BLOCK)


def face_rims(field):
    return with_halo(field, (("gx", 1), ("gy", 2)), 1)


def corner_rims(field):
    return with_halo(field, (("gx", 1), ("gy", 2)), 1)


def shards(
    net_inputs,
    velocity,
    particle_mass,
    block_column,
    cell_height,
    block_counts,
    cotangent,
    input_weight,
    input_bias,
    middle_weight,
    middle_bias,
    output_weight,
    output_bias,
):
    params = (input_weight, input_bias, middle_weight, middle_bias, output_weight, output_bias)
    tiles_x = lax.axis_size("gx")
    tiles_y = lax.axis_size("gy")
    index_x = lax.axis_index("gx")
    index_y = lax.axis_index("gy")
    width_x = CX * tiles_x
    width_y = CY * tiles_y
    live_count = block_counts[index_x * tiles_y + index_y]
    block_live = (jnp.arange(PB, dtype=jnp.int32) < live_count).astype(jnp.float32)
    live_mask = jnp.repeat(block_live, BLOCK)
    weight = particle_mass * live_mask
    global_x = block_column // width_y
    global_y = block_column % width_y
    local_x = (global_x - index_x * CX + 1) % width_x
    local_y = (global_y - index_y * CY + 1) % width_y
    block_ext = local_x * (CY + 2) + local_y
    group_span = GROUP * BLOCK
    turn_count = PB // GROUP

    def forward_turn(turn_index, stress_acc):
        start = turn_index * group_span
        input_piece = lax.dynamic_slice_in_dim(net_inputs, start, group_span, 1)
        stress_piece = network(input_piece, *params)[4]
        return lax.dynamic_update_slice_in_dim(stress_acc, stress_piece, start, 1)

    stress = lax.fori_loop(0, turn_count, forward_turn, jnp.zeros((9, PB * BLOCK), jnp.float32))
    values = jnp.concatenate([weight * velocity, weight[None], weight * stress, cotangent], axis=0)
    totals = fold_deposit(values, cell_height, block_ext)
    inverse = 1.0 / (totals[3] + 1.0)
    drift = totals[0:3] * inverse
    velocity_cot = totals[13:16]
    energy = lax.psum(jnp.sum(drift * drift), ("gx", "gy")) / (width_x * width_y * NZ)
    step_size = time_scale / jnp.sqrt(energy + epsilon)
    force = divergence(face_rims(totals[4:13]))
    velocity_ext = corner_rims(drift + step_size * inverse * force)
    force_cot = step_size * inverse * velocity_cot
    stress_ext = corner_rims(stress_adjoint(face_rims(force_cot)))
    new_velocity = read_cells(velocity_ext, cell_height, block_ext)
    stress_cot = read_cells(stress_ext, cell_height, block_ext) * weight

    def backward_turn(turn_index, running):
        start = turn_index * group_span
        input_piece = lax.dynamic_slice_in_dim(net_inputs, start, group_span, 1)
        cot_piece = lax.dynamic_slice_in_dim(stress_cot, start, group_span, 1)
        fresh_grads = network_grads(input_piece, cot_piece, *params)
        return tuple(
            (earlier_term + later_term for earlier_term, later_term in zip(running, fresh_grads))
        )

    hidden_units = input_weight.shape[0]
    input_rows = input_weight.shape[1]
    initial = (
        jnp.zeros((hidden_units, input_rows), jnp.float32),
        jnp.zeros((hidden_units,), jnp.float32),
        jnp.zeros((hidden_units, hidden_units), jnp.float32),
        jnp.zeros((hidden_units,), jnp.float32),
        jnp.zeros((9, hidden_units), jnp.float32),
        jnp.zeros((9,), jnp.float32),
    )
    local_grads = lax.fori_loop(0, turn_count, backward_turn, initial)
    grad_first_w, grad_first_b, grad_mid_w, grad_mid_b, grad_out_w, grad_out_b = local_grads
    summed = lax.psum(
        (grad_first_w, grad_first_b, grad_mid_w, grad_mid_b, grad_out_w, grad_out_b), ("gx", "gy")
    )
    live_total = jnp.sum(block_counts).astype(jnp.float32) * BLOCK
    root_total = jnp.sqrt(live_total)
    return (
        new_velocity,
        summed[0] / root_total,
        summed[1] / root_total,
        summed[2] / root_total,
        summed[3] / root_total,
        summed[4] / root_total,
        summed[5] / root_total,
    )


def solution(mesh):
    return jax.shard_map(
        shards,
        mesh=mesh,
        in_specs=(
            P(None, ("gx", "gy")),
            P(None, ("gx", "gy")),
            P(("gx", "gy")),
            P(("gx", "gy")),
            P(("gx", "gy")),
            P(),
            P(None, ("gx", "gy")),
            P(),
            P(),
            P(),
            P(),
            P(),
            P(),
        ),
        out_specs=(P(None, ("gx", "gy")), P(), P(), P(), P(), P(), P()),
        check_vma=False,
    )
```

profile of v0, /device:TPU:1, one launch (start us, length us, event | category | flops | bytes accessed | tf_op | source)
XLA Modules:
  0.0 457.0 jit_solution(10183096604640903412)
XLA Ops:
  2.9 33.2 %while.77 = (s32[]{:T(128)}, f32[9,49152]{1,0:T(8,128)S(1)}, bf16[25,49152]{1,0:T(8,128)(2,1)}, bf16[80,25]{0,1:T(8,128)(2,1)S(1)}, f32[80]{0:T(128)S(1)}, /*ind...) while((s32[]{:T(128)}, f32[9,49152]{1,0:T(8,128)S(1)}, ...), condition=%wide.region_1.2_spmd, body=%wide.region_0.1_spmd.sunk | while | flops 157360128 | bytes 3700115 | solution.py:209
  2.9 3.1 multiply_convert_fusion.13
  8.5 3.1 multiply_convert_fusion.13
  14.0 3.1 multiply_convert_fusion.13
  19.5 3.1 multiply_convert_fusion.13
  25.0 3.1 multiply_convert_fusion.13
  30.6 3.1 multiply_convert_fusion.13
  38.6 33.5 %while.78 = (s32[]{:T(128)}, f32[6,64,16,128]{3,2,1,0:T(8,128)}, s32[6]{0:T(128)S(1)}, f32[16,49152]{1,0:T(8,128)S(1)}, s32[49152]{0:T(1024)}, /*index=5*/s32[]{:T(128)}, s32[1]{0:T(128)}, s32[]{:T(128)}, s32[]{:T(128)}) while((s32[]{:T(128)}, f32[6,64,16,128]{3,2,1,0:T(8,128)}, s32[6]{0:T(128)S(1)}, f32[16,49152]{1,0:T(8,128)S(1)}, ...), condition=%wide.region_3.4_spmd, body=%wide.region_2.3_spmd.sunk | while | flops 202375168 | bytes 1147551 | solution.py:131
  40.6 3.6 fusion.132
  46.2 3.6 fusion.132
  51.8 3.6 fusion.132
  57.4 3.6 fusion.132
  62.9 3.6 fusion.132
  68.5 3.6 fusion.132
  72.9 30.5 %scatter_fusion = f32[324,16,128]{2,1,0:T(8,128)S(1)} fusion(f32[324,16,128]{2,1,0:T(8,128)S(1)} %broadcast_in_dim.91, s32[384]{0:T(512)S(1)} %get-tuple-element.809, f32[384,16,128]{2,1,0:T(8,128)} %bitcast.182), kind=kCustom, calls=%fused_computation.2 | custom fusion | flops 786432 | bytes 9438720 | tf_op jit(solution)/shard_map/scatter-add | solution.py:135
  103.4 2.7 collective-permute-start
  108.3 3.5 collective-permute-done.1
  116.5 3.3 collective-permute-done.2
  119.7 3.5 collective-permute-done.3
  126.3 38.7 %psum.49 = f32[]{:T(128)} all-reduce(f32[]{:T(128)} %multiply_reduce_fusion), channel_id=1, replica_groups=mesh['gx'=8,'gy'=4] {'gx','gy'}, use_global_device_ids=true, to_apply=%region_6.7 | all-reduce | flops 1 | bytes 8 | tf_op jit(solution)/shard_map/psum | solution.py:215
  168.6 2.5 collective-permute-done.6
  171.1 3.6 collective-permute-done.7
  177.6 4.9 %collective-permute-start.12 = (f32[3,1,16,128]{3,0,2,1:T(4,128)S(1)}, f32[3,1,16,128]{3,0,2,1:T(4,128)S(1)}, u32[]{:S(2)}, u32[]{:S(2)}) collective-permute-start(f32[3,1,16,128]{3,0,2,1:T(4,128)S(1)} %get-tuple-element.843), channel_id=1, source_target_pairs={{0,4},{4,8},{8,12},{12,16},{16,20},{20,24},{24,28},{28,0},{1,5},{5... | collective-permute-start | bytes 73736 | tf_op jit(solution)/shard_map/ppermute | solution.py:25
  199.8 52.2 %while.79 = (s32[]{:T(128)}, f32[6,3,8192]{2,1,0:T(4,128)}, s32[6]{0:T(128)S(1)}, s32[49152]{0:T(1024)}, s32[384]{0:T(512)}, /*index=5*/f32[3,324,128]{2,0,1:T(4...) while((s32[]{:T(128)}, f32[6,3,8192]{2,1,0:T(4,128)}, ...), condition=%wide.region_8.9_spmd, body=%wide.region_7.8_spmd.sunk | while | flops 38798536 | bytes 530149 | solution.py:157
  203.9 4.6 %fusion.134 = f32[6,3,8192]{2,1,0:T(4,128)} fusion(f32[6,3,8192]{2,1,0:T(4,128)} %get-tuple-element.1189, s32[]{:T(128)} %get-tuple-element.1188, s32[64,128]{1,0:T(8,128)S(1)} %dynamic-slice_bitcast_fusion.12, f32[64,3,128]{2,1,0:T(4,128)S(1)} %gather_fusion), kind=kOutput, calls=%fused_computation.27.clone.1 | convolution fusion | flops 38797312 | bytes 262656 | tf_op jit(solution)/shard_map/while/body/eval_jaxpr/cbz,bpz->cbp/dot_general | solution.py:154
  212.6 4.6 %fusion.134 = f32[6,3,8192]{2,1,0:T(4,128)} fusion(f32[6,3,8192]{2,1,0:T(4,128)} %get-tuple-element.1189, s32[]{:T(128)} %get-tuple-element.1188, s32[64,128]{1,0:T(8,128)S(1)} %dynamic-slice_bitcast_fusion.12, f32[64,3,128]{2,1,0:T(4,128)S(1)} %gather_fusion), kind=kOutput, calls=%fused_computation.27.clone.1 | convolution fusion | flops 38797312 | bytes 262656 | tf_op jit(solution)/shard_map/while/body/eval_jaxpr/cbz,bpz->cbp/dot_general | solution.py:154
  221.3 4.6 %fusion.134 = f32[6,3,8192]{2,1,0:T(4,128)} fusion(f32[6,3,8192]{2,1,0:T(4,128)} %get-tuple-element.1189, s32[]{:T(128)} %get-tuple-element.1188, s32[64,128]{1,0:T(8,128)S(1)} %dynamic-slice_bitcast_fusion.12, f32[64,3,128]{2,1,0:T(4,128)S(1)} %gather_fusion), kind=kOutput, calls=%fused_computation.27.clone.1 | convolution fusion | flops 38797312 | bytes 262656 | tf_op jit(solution)/shard_map/while/body/eval_jaxpr/cbz,bpz->cbp/dot_general | solution.py:154
  230.0 4.6 %fusion.134 = f32[6,3,8192]{2,1,0:T(4,128)} fusion(f32[6,3,8192]{2,1,0:T(4,128)} %get-tuple-element.1189, s32[]{:T(128)} %get-tuple-element.1188, s32[64,128]{1,0:T(8,128)S(1)} %dynamic-slice_bitcast_fusion.12, f32[64,3,128]{2,1,0:T(4,128)S(1)} %gather_fusion), kind=kOutput, calls=%fused_computation.27.clone.1 | convolution fusion | flops 38797312 | bytes 262656 | tf_op jit(solution)/shard_map/while/body/eval_jaxpr/cbz,bpz->cbp/dot_general | solution.py:154
  238.7 4.6 %fusion.134 = f32[6,3,8192]{2,1,0:T(4,128)} fusion(f32[6,3,8192]{2,1,0:T(4,128)} %get-tuple-element.1189, s32[]{:T(128)} %get-tuple-element.1188, s32[64,128]{1,0:T(8,128)S(1)} %dynamic-slice_bitcast_fusion.12, f32[64,3,128]{2,1,0:T(4,128)S(1)} %gather_fusion), kind=kOutput, calls=%fused_computation.27.clone.1 | convolution fusion | flops 38797312 | bytes 262656 | tf_op jit(solution)/shard_map/while/body/eval_jaxpr/cbz,bpz->cbp/dot_general | solution.py:154
  247.4 4.6 %fusion.134 = f32[6,3,8192]{2,1,0:T(4,128)} fusion(f32[6,3,8192]{2,1,0:T(4,128)} %get-tuple-element.1189, s32[]{:T(128)} %get-tuple-element.1188, s32[64,128]{1,0:T(8,128)S(1)} %dynamic-slice_bitcast_fusion.12, f32[64,3,128]{2,1,0:T(4,128)S(1)} %gather_fusion), kind=kOutput, calls=%fused_computation.27.clone.1 | convolution fusion | flops 38797312 | bytes 262656 | tf_op jit(solution)/shard_map/while/body/eval_jaxpr/cbz,bpz->cbp/dot_general | solution.py:154
  253.5 62.8 %while.80 = (s32[]{:T(128)}, f32[6,9,8192]{2,1,0:T(8,128)}, s32[6]{0:T(128)}, s32[49152]{0:T(1024)}, s32[384]{0:T(512)}, /*index=5*/f32[9,324,128]{2,0,1:T(8,128...) while((s32[]{:T(128)}, f32[6,9,8192]{2,1,0:T(8,128)}, ...), condition=%wide.region_10.11_spmd, body=%wide.region_9.10_spmd.sunk | while | flops 114296008 | bytes 3282661 | solution.py:157
  258.2 4.7 %fusion.136 = f32[9,64,128]{2,0,1:T(8,128)S(1)} fusion(s32[64,128]{1,0:T(8,128)S(1)} %dynamic-slice_bitcast_fusion.13, f32[64,9,128]{2,1,0:T(8,128)S(1)} %gather_fusion.1), kind=kOutput, calls=%fused_computation.37.clone.1 | convolution fusion | flops 114294784 | bytes 622592 | tf_op jit(solution)/shard_map/while/body/eval_jaxpr/cbz,bpz->cbp/dot_general | solution.py:154
  268.7 4.7 %fusion.136 = f32[9,64,128]{2,0,1:T(8,128)S(1)} fusion(s32[64,128]{1,0:T(8,128)S(1)} %dynamic-slice_bitcast_fusion.13, f32[64,9,128]{2,1,0:T(8,128)S(1)} %gather_fusion.1), kind=kOutput, calls=%fused_computation.37.clone.1 | convolution fusion | flops 114294784 | bytes 622592 | tf_op jit(solution)/shard_map/while/body/eval_jaxpr/cbz,bpz->cbp/dot_general | solution.py:154
  279.2 4.7 %fusion.136 = f32[9,64,128]{2,0,1:T(8,128)S(1)} fusion(s32[64,128]{1,0:T(8,128)S(1)} %dynamic-slice_bitcast_fusion.13, f32[64,9,128]{2,1,0:T(8,128)S(1)} %gather_fusion.1), kind=kOutput, calls=%fused_computation.37.clone.1 | convolution fusion | flops 114294784 | bytes 622592 | tf_op jit(solution)/shard_map/while/body/eval_jaxpr/cbz,bpz->cbp/dot_general | solution.py:154
  289.6 4.7 %fusion.136 = f32[9,64,128]{2,0,1:T(8,128)S(1)} fusion(s32[64,128]{1,0:T(8,128)S(1)} %dynamic-slice_bitcast_fusion.13, f32[64,9,128]{2,1,0:T(8,128)S(1)} %gather_fusion.1), kind=kOutput, calls=%fused_computation.37.clone.1 | convolution fusion | flops 114294784 | bytes 622592 | tf_op jit(solution)/shard_map/while/body/eval_jaxpr/cbz,bpz->cbp/dot_general | solution.py:154
  300.1 4.7 %fusion.136 = f32[9,64,128]{2,0,1:T(8,128)S(1)} fusion(s32[64,128]{1,0:T(8,128)S(1)} %dynamic-slice_bitcast_fusion.13, f32[64,9,128]{2,1,0:T(8,128)S(1)} %gather_fusion.1), kind=kOutput, calls=%fused_computation.37.clone.1 | convolution fusion | flops 114294784 | bytes 622592 | tf_op jit(solution)/shard_map/while/body/eval_jaxpr/cbz,bpz->cbp/dot_general | solution.py:154
  310.6 4.7 %fusion.136 = f32[9,64,128]{2,0,1:T(8,128)S(1)} fusion(s32[64,128]{1,0:T(8,128)S(1)} %dynamic-slice_bitcast_fusion.13, f32[64,9,128]{2,1,0:T(8,128)S(1)} %gather_fusion.1), kind=kOutput, calls=%fused_computation.37.clone.1 | convolution fusion | flops 114294784 | bytes 622592 | tf_op jit(solution)/shard_map/while/body/eval_jaxpr/cbz,bpz->cbp/dot_general | solution.py:154
  316.3 3.0 copy.46
  323.4 90.2 %while.81 = (s32[]{:T(128)}, f32[80,25]{0,1:T(8,128)S(1)}, f32[80]{0:T(128)S(1)}, f32[80,80]{1,0:T(8,128)S(1)}, f32[80]{0:T(128)S(1)}, /*index=5*/f32[9,80]{1,0:...) while((s32[]{:T(128)}, f32[80,25]{0,1:T(8,128)S(1)}, ...), condition=%wide.region_15.16_spmd.clone, body=%wide.region_11.15_spmd.clone.sunk | while | flops 428042240 | bytes 53093524 | solution.py:243
  326.0 3.9 fusion.148
  341.1 3.9 fusion.148
  344.9 2.4 convolution_add_fusion.7
  356.1 3.9 fusion.148
  371.1 3.9 fusion.148
  375.0 2.4 convolution_add_fusion.7
  386.2 3.9 fusion.148
  401.2 3.9 fusion.148
  413.6 40.5 %all-reduce.2 = (f32[80,25]{0,1:T(8,128)S(1)}, f32[80]{0:T(128)S(1)}, f32[80,80]{1,0:T(8,128)S(1)}, f32[80]{0:T(128)S(1)}, f32[9,80]{1,0:T(8,128)S(1)}, /*index=5*/f32[9]{0:T(128)S(1)}) all-reduce(f32[80,25]{0,1:T(8,128)S(1)} %get-tuple-element.666, f32[80]{0:T(128)S(1)} %get-tuple-element.667, ...), channel_id=1, replica_groups=mesh['gx'=8,'gy'=4] {'gx','gy'}, use_global_device_ids=true, to_apply=%region_16.17 | all-reduce | flops 9289 | bytes 74312 | tf_op jit(solution)/shard_map/psum | solution.py:245
  (314 shorter events, 173.1 us)
Async XLA Ops:
  0.6 2.2 copy-start.4
  0.6 2.2 copy-start.6
  0.7 2.2 copy-start.9
  0.7 2.2 copy-start.15
  0.7 2.2 copy-start.11
  0.7 2.2 copy-start.13
  2.9 33.2 %copy-start.5 = (f32[49152]{0:T(1024)S(1)}, f32[49152]{0:T(1024)}, u32[]{:S(2)}) copy-start(f32[49152]{0:T(1024)} %param.33) | copy-start | bytes 589828
  38.6 33.5 %copy-start.8 = (s32[384]{0:T(512)S(1)}, s32[384]{0:T(512)}, u32[]{:S(2)}) copy-start(s32[384]{0:T(512)} %param.34) | copy-start | bytes 4612
  103.4 11.7 %copy-start.14 = (s32[32]{0:T(128)S(1)}, s32[32]{0:T(128)}, u32[]{:S(2)}) copy-start(s32[32]{0:T(128)} %param.36) | copy-start | bytes 388
  103.4 4.8 %collective-permute-start = (f32[16,1,18,128]{3,0,2,1:T(8,128)S(1)}, f32[16,1,18,128]{3,0,2,1:T(8,128)S(1)}, u32[]{:S(2)}, u32[]{:S(2)}) collective-permute-start(f32[16,1,18,128]{3,0,2,1:T(8,128)S(1)} %get-tuple-element.819), channel_id=1, source_target_pairs={{0,4},{4,8},{8,12},{12,16},{16,20},{20,24},{24,28},{28,0},{1,5},{5... | collective-permute-start | bytes 442376 | tf_op jit(solution)/shard_map/ppermute | solution.py:25
  106.2 5.6 %collective-permute-start.1 = (f32[16,1,18,128]{3,0,2,1:T(8,128)S(1)}, f32[16,1,18,128]{3,0,2,1:T(8,128)S(1)}, u32[]{:S(2)}, u32[]{:S(2)}) collective-permute-start(f32[16,1,18,128]{3,0,2,1:T(8,128)S(1)} %get-tuple-element.820), channel_id=1, source_target_pairs={{4,0},{8,4},{12,8},{16,12},{20,16},{24,20},{28,24},{0,28},{5,1},{9... | collective-permute-start | bytes 442376 | tf_op jit(solution)/shard_map/ppermute | solution.py:26
  112.5 7.3 %collective-permute-start.2 = (f32[16,20,1,128]{3,0,2,1:T(8,128)}, f32[16,20,1,128]{3,0,2,1:T(8,128)S(1)}, u32[]{:S(2)}, u32[]{:S(2)}) collective-permute-start(f32[16,20,1,128]{3,0,2,1:T(8,128)} %get-tuple-element.817), channel_id=1, source_target_pairs={{0,1},{1,2},{2,3},{3,0},{4,5},{5,6},{6,7},{7,4},{8,9},{9,10},{10,1... | collective-permute-start | bytes 491528 | tf_op jit(solution)/shard_map/ppermute | solution.py:25
  114.1 9.1 %collective-permute-start.3 = (f32[16,20,1,128]{3,0,2,1:T(8,128)S(1)}, f32[16,20,1,128]{3,0,2,1:T(8,128)S(1)}, u32[]{:S(2)}, u32[]{:S(2)}) collective-permute-start(f32[16,20,1,128]{3,0,2,1:T(8,128)S(1)} %get-tuple-element.818), channel_id=1, source_target_pairs={{1,0},{2,1},{3,2},{0,3},{5,4},{6,5},{7,6},{4,7},{9,8},{10,9},{11,1... | collective-permute-start | bytes 491528 | tf_op jit(solution)/shard_map/ppermute | solution.py:26
  124.2 41.9 %collective-permute-start.4 = (f32[9,1,16,128]{3,0,2,1:T(8,128)S(1)}, f32[9,1,16,128]{3,0,2,1:T(8,128)S(1)}, u32[]{:S(2)}, u32[]{:S(2)}) collective-permute-start(f32[9,1,16,128]{3,0,2,1:T(8,128)S(1)} %get-tuple-element.825), channel_id=1, source_target_pairs={{0,4},{4,8},{8,12},{12,16},{16,20},{20,24},{24,28},{28,0},{1,5},{5... | collective-permute-start | bytes 221192 | tf_op jit(solution)/shard_map/ppermute | solution.py:25
  126.3 39.8 %collective-permute-start.5 = (f32[9,1,16,128]{3,0,2,1:T(8,128)S(1)}, f32[9,1,16,128]{3,0,2,1:T(8,128)S(1)}, u32[]{:S(2)}, u32[]{:S(2)}) collective-permute-start(f32[9,1,16,128]{3,0,2,1:T(8,128)S(1)} %get-tuple-element.826), channel_id=1, source_target_pairs={{4,0},{8,4},{12,8},{16,12},{20,16},{24,20},{28,24},{0,28},{5,1},{9... | collective-permute-start | bytes 221192 | tf_op jit(solution)/shard_map/ppermute | solution.py:26
  166.1 4.9 %collective-permute-start.6 = (f32[9,18,1,128]{3,0,2,1:T(8,128)S(1)}, f32[9,18,1,128]{3,0,2,1:T(8,128)S(1)}, u32[]{:S(2)}, u32[]{:S(2)}) collective-permute-start(f32[9,18,1,128]{3,0,2,1:T(8,128)S(1)} %get-tuple-element.821), channel_id=1, source_target_pairs={{0,1},{1,2},{2,3},{3,0},{4,5},{5,6},{6,7},{7,4},{8,9},{9,10},{10,1... | collective-permute-start | bytes 248840 | tf_op jit(solution)/shard_map/ppermute | solution.py:25
  168.2 6.5 %collective-permute-start.7 = (f32[9,18,1,128]{3,0,2,1:T(8,128)S(1)}, f32[9,18,1,128]{3,0,2,1:T(8,128)S(1)}, u32[]{:S(2)}, u32[]{:S(2)}) collective-permute-start(f32[9,18,1,128]{3,0,2,1:T(8,128)S(1)} %get-tuple-element.822), channel_id=1, source_target_pairs={{1,0},{2,1},{3,2},{0,3},{5,4},{6,5},{7,6},{4,7},{9,8},{10,9},{11,1... | collective-permute-start | bytes 248840 | tf_op jit(solution)/shard_map/ppermute | solution.py:26
  177.6 6.8 %collective-permute-start.12 = (f32[3,1,16,128]{3,0,2,1:T(4,128)S(1)}, f32[3,1,16,128]{3,0,2,1:T(4,128)S(1)}, u32[]{:S(2)}, u32[]{:S(2)}) collective-permute-start(f32[3,1,16,128]{3,0,2,1:T(4,128)S(1)} %get-tuple-element.843), channel_id=1, source_target_pairs={{0,4},{4,8},{8,12},{12,16},{16,20},{20,24},{24,28},{28,0},{1,5},{5... | collective-permute-start | bytes 73736 | tf_op jit(solution)/shard_map/ppermute | solution.py:25
  182.5 3.3 collective-permute-start.13
  182.5 5.8 %collective-permute-start.8 = (f32[3,1,16,128]{3,0,2,1:T(4,128)S(1)}, f32[3,1,16,128]{3,0,2,1:T(4,128)S(1)}, u32[]{:S(2)}, u32[]{:S(2)}) collective-permute-start(f32[3,1,16,128]{3,0,2,1:T(4,128)S(1)} %get-tuple-element.845), channel_id=1, source_target_pairs={{0,4},{4,8},{8,12},{12,16},{16,20},{20,24},{24,28},{28,0},{1,5},{5... | collective-permute-start | bytes 73736 | tf_op jit(solution)/shard_map/ppermute | solution.py:25
  184.3 4.0 collective-permute-start.9
  185.9 4.9 %collective-permute-start.14 = (f32[3,18,1,128]{3,0,2,1:T(4,128)S(1)}, f32[3,18,1,128]{3,0,2,1:T(4,128)S(1)}, u32[]{:S(2)}, u32[]{:S(2)}) collective-permute-start(f32[3,18,1,128]{3,0,2,1:T(4,128)S(1)} %get-tuple-element.838), channel_id=1, source_target_pairs={{0,1},{1,2},{2,3},{3,0},{4,5},{5,6},{6,7},{7,4},{8,9},{9,10},{10,1... | collective-permute-start | bytes 82952 | tf_op jit(solution)/shard_map/ppermute | solution.py:25
  186.7 4.0 collective-permute-start.15
  188.3 6.7 %collective-permute-start.10 = (f32[3,18,1,128]{3,0,2,1:T(4,128)S(1)}, f32[3,18,1,128]{3,0,2,1:T(4,128)S(1)}, u32[]{:S(2)}, u32[]{:S(2)}) collective-permute-start(f32[3,18,1,128]{3,0,2,1:T(4,128)S(1)} %get-tuple-element.840), channel_id=1, source_target_pairs={{0,1},{1,2},{2,3},{3,0},{4,5},{5,6},{6,7},{7,4},{8,9},{9,10},{10,1... | collective-permute-start | bytes 82952 | tf_op jit(solution)/shard_map/ppermute | solution.py:25
  188.8 6.2 %collective-permute-start.11 = (f32[3,18,1,128]{3,0,2,1:T(4,128)S(1)}, f32[3,18,1,128]{3,0,2,1:T(4,128)S(1)}, u32[]{:S(2)}, u32[]{:S(2)}) collective-permute-start(f32[3,18,1,128]{3,0,2,1:T(4,128)S(1)} %get-tuple-element.841), channel_id=1, source_target_pairs={{1,0},{2,1},{3,2},{0,3},{5,4},{6,5},{7,6},{4,7},{9,8},{10,9},{11,1... | collective-permute-start | bytes 82952 | tf_op jit(solution)/shard_map/ppermute | solution.py:26
  192.1 3.5 collective-permute-start.16
  193.5 3.8 collective-permute-start.17
  197.4 54.6 %collective-permute-start.18 = (f32[9,18,1,128]{3,2,1,0:T(1,128)S(1)}, f32[9,18,1,128]{3,2,1,0:T(1,128)S(1)}, u32[]{:S(2)}, u32[]{:S(2)}) collective-permute-start(f32[9,18,1,128]{3,2,1,0:T(1,128)S(1)} %get-tuple-element.832), channel_id=1, source_target_pairs={{0,1},{1,2},{2,3},{3,0},{4,5},{5,6},{6,7},{7,4},{8,9},{9,10},{10,1... | collective-permute-start | bytes 248840 | tf_op jit(solution)/shard_map/ppermute | solution.py:25
  197.5 54.6 %collective-permute-start.19 = (f32[9,18,1,128]{3,2,1,0:T(1,128)S(1)}, f32[9,18,1,128]{3,2,1,0:T(1,128)S(1)}, u32[]{:S(2)}, u32[]{:S(2)}) collective-permute-start(f32[9,18,1,128]{3,2,1,0:T(1,128)S(1)} %get-tuple-element.833), channel_id=1, source_target_pairs={{1,0},{2,1},{3,2},{0,3},{5,4},{6,5},{7,6},{4,7},{9,8},{10,9},{11,1... | collective-permute-start | bytes 248840 | tf_op jit(solution)/shard_map/ppermute | solution.py:26
  321.4 1.9 copy-start.7
  326.0 3.9 copy-start.17
  329.9 2.5 copy-start.19
  332.4 3.0 copy-start.18
  341.0 3.9 copy-start.17
  344.9 2.5 copy-start.19
  347.4 3.0 copy-start.18
  356.1 3.9 copy-start.17
  360.0 2.5 copy-start.19
  362.4 3.0 copy-start.18
  371.1 3.9 copy-start.17
  375.0 2.5 copy-start.19
  377.5 3.0 copy-start.18
  386.2 3.9 copy-start.17
  390.0 2.5 copy-start.19
  392.5 3.0 copy-start.18
  401.2 3.9 copy-start.17
  405.1 2.5 copy-start.19
  407.5 3.0 copy-start.18
  (7 other events, 11.7 us)
where the time goes:
time: 463 us; the launch traced here: 457 us
  matrix products  193 us (42%)
  blocking collectives  79.2 us (17%)
  other arithmetic  61.4 us (13%)
  local copies, waits for them, and re-layouts  52.5 us (11%)
  starting transfers between devices  25.9 us (6%)
  waiting for transfers between devices  22.2 us (5%)
  loops' own time  20.5 us (4%)
    dot_general x12, matrix products, group_read(): jnp.einsum('cbz,bpz->cbp', column_rows, selector, precision=lax.Precision...  56.1 us
    psum x1, blocking collectives, shards(): lax.psum((grad_first_w, grad_first_b, grad_mid_w, grad_mid_b, grad_out_w,...  40.5 us
    psum x1, blocking collectives, shards(): lax.psum(jnp.sum(drift * drift), ('gx', 'gy')) / (width_x * width_y * NZ)  38.7 us
    scatter-add x1, other arithmetic, fold_deposit(): jnp.zeros(((CX + 2) * (CY + 2), channels, NZ), jnp.float32).at[block_ext]  30.5 us
    dot_general x12, matrix products, network(): jnp.dot(input_weight, inputs, preferred_element_type=jnp.float32)  28.1 us
    dot_general x6, matrix products, network_grads(): jnp.dot(output_weight.T, stress_cot_low, preferred_element_type=jnp.float32)  23.1 us
    dot_general x6, matrix products, group_sums(): jnp.einsum('cbp,bpz->bcz', piece_values, selector, precision=lax.Precisio...  21.4 us
    ppermute x10, starting transfers between devices, with_halo(): before = lax.ppermute(last, axis, up)  17.3 us
  transfers between devices with their start and end apart: 20, of which 9 were waited for; matrix products, arithmetic and copies ran while one was open for 10% of the time, Pallas kernels for 0%

commit v1 on v0

v1 whole, which is shorter than its diff:
```python
import jax
import jax.numpy as jnp
from jax import lax
from jax.experimental import pallas as pl
from jax.experimental.pallas import tpu as pltpu
from jax.sharding import PartitionSpec as P

CX = 16
CY = 16
NZ = 128
PB = 384
BLOCK = 128
GROUP = 16
ROWS = 16
SPAN = GROUP * BLOCK


time_scale = 0.5
epsilon = 1e-06


def sigmoid(values):
    return 0.5 * jnp.tanh(0.5 * values) + 0.5


def dot(left, right):
    return jnp.dot(left, right, preferred_element_type=jnp.float32)


def dot_nt(left, right):
    return lax.dot_general(
        left, right, (((1,), (1,)), ((), ())), preferred_element_type=jnp.float32
    )


def split_halves(values):
    high = values.astype(jnp.bfloat16)
    low = (values - high.astype(jnp.float32)).astype(jnp.bfloat16)
    return jnp.concatenate([high, low], axis=0)


def height_selector(heights):
    level = lax.broadcasted_iota(jnp.int32, (NZ, BLOCK), 0)
    return jnp.where(level == heights, 1.0, 0.0).astype(jnp.bfloat16)


def deposit_kernel(
    column_ref,
    live_ref,
    inputs_ref,
    velocity_ref,
    mass_ref,
    height_ref,
    cot_ref,
    w1_ref,
    b1_ref,
    w2_ref,
    b2_ref,
    w3_ref,
    b3_ref,
    sums_ref,
):
    turn = pl.program_id(0)

    @pl.when(turn == 0)
    def _():
        sums_ref[...] = jnp.zeros_like(sums_ref)

    first = dot(w1_ref[...], inputs_ref[...]) + b1_ref[...]
    first_act = (first * sigmoid(first)).astype(jnp.bfloat16)
    second = dot(w2_ref[...], first_act) + b2_ref[...]
    second_act = (second * sigmoid(second)).astype(jnp.bfloat16)
    stress = dot(w3_ref[...], second_act) + b3_ref[...]
    gap = jnp.zeros((ROWS - 6, SPAN), jnp.float32)
    values = stress + jnp.concatenate([velocity_ref[...], gap, cot_ref[...]], axis=0)
    weighted = lax.broadcasted_iota(jnp.int32, (ROWS, BLOCK), 0) < 13
    for block in range(GROUP):
        index = turn * GROUP + block
        live = jnp.where(index < live_ref[0], 1.0, 0.0)
        weight = mass_ref[block : block + 1, :] * live
        piece = values[:, block * BLOCK : (block + 1) * BLOCK] * jnp.where(weighted, weight, 1.0)
        selector = height_selector(height_ref[block : block + 1, :])
        both = dot_nt(split_halves(piece), selector)
        column = column_ref[index]
        sums_ref[column] = sums_ref[column] + (both[:ROWS] + both[ROWS:])


def fill_grid(step, wide_ref, scaled_ref, grid_ref):
    wide_x, wide_y = CX + 4, CY + 4
    cots = lax.broadcasted_iota(jnp.int32, (wide_y, ROWS, NZ), 1) >= 13
    lane = lax.broadcasted_iota(jnp.int32, (CY + 2, ROWS, NZ), 2)

    def scale_row(x, carry):
        totals = wide_ref[x]
        inverse = 1.0 / (totals[:, 3:4] + 1.0)
        scaled_ref[x] = totals * jnp.where(cots, inverse, 1.0)
        return carry

    lax.fori_loop(0, wide_x, scale_row, 0)

    def fill_row(x, carry):
        here = scaled_ref[x + 1]
        middle = here[1:-1]
        diff_x = 0.5 * (scaled_ref[x + 2, 1 : wide_y - 1] - scaled_ref[x, 1 : wide_y - 1])
        diff_y = 0.5 * (here[2:] - here[:-2])
        above = jnp.where(lane < NZ - 1, pltpu.roll(middle, NZ - 1, 2), 0.0)
        below = jnp.where(lane > 0, pltpu.roll(middle, 1, 2), 0.0)
        diff_z = 0.5 * (above - below)
        inverse = 1.0 / (middle[:, 3:4] + 1.0)
        force = diff_x[:, 4:7] + diff_y[:, 7:10] + diff_z[:, 10:13]
        speed = inverse * middle[:, 0:3] + step * (inverse * force)
        cot_rows = [-step * diff[:, 13:16] for diff in (diff_x, diff_y, diff_z)]
        rows = jnp.concatenate(
            [speed, jnp.zeros_like(inverse)] + cot_rows + [jnp.zeros_like(speed)], axis=1
        )
        grid_ref[pl.ds(x * (CY + 2), CY + 2)] = rows
        return carry

    lax.fori_loop(0, CX + 2, fill_row, 0)


def gather_kernel(
    column_ref,
    live_ref,
    step_ref,
    inputs_ref,
    mass_ref,
    height_ref,
    wide_ref,
    w1_ref,
    b1_ref,
    w2_ref,
    b2_ref,
    w3t_ref,
    w2t_ref,
    velocity_ref,
    gin_ref,
    gmid_ref,
    gout_ref,
    bin_ref,
    bmid_ref,
    bout_ref,
    scaled_ref,
    grid_ref,
):
    turn = pl.program_id(0)
    step = step_ref[0]

    @pl.when(turn == 0)
    def _():
        for ref in (gin_ref, gmid_ref, gout_ref, bin_ref, bmid_ref, bout_ref):
            ref[...] = jnp.zeros_like(ref)
        fill_grid(step, wide_ref, scaled_ref, grid_ref)

    picked_cols, cot_cols = [], []
    for block in range(GROUP):
        index = turn * GROUP + block
        live = jnp.where(index < live_ref[0], 1.0, 0.0)
        weight = mass_ref[block : block + 1, :] * live
        selector = height_selector(height_ref[block : block + 1, :])
        both = dot(split_halves(grid_ref[column_ref[index]]), selector)
        picked = both[:ROWS] + both[ROWS:]
        picked_cols.append(picked)
        cot_cols.append(picked * weight)
    picked = jnp.concatenate(picked_cols, axis=1)
    stress_cot = jnp.concatenate(cot_cols, axis=1)
    velocity_ref[...] = picked[0:3]

    inputs = inputs_ref[...]
    first = dot(w1_ref[...], inputs) + b1_ref[...]
    first_sig = sigmoid(first)
    first_act = (first * first_sig).astype(jnp.bfloat16)
    second = dot(w2_ref[...], first_act) + b2_ref[...]
    second_sig = sigmoid(second)
    second_act = (second * second_sig).astype(jnp.bfloat16)
    cot_low = stress_cot.astype(jnp.bfloat16)
    second_cot = dot(w3t_ref[...], cot_low) * (second_sig * (1.0 + second * (1.0 - second_sig)))
    second_low = second_cot.astype(jnp.bfloat16)
    first_cot = dot(w2t_ref[...], second_low) * (first_sig * (1.0 + first * (1.0 - first_sig)))
    first_low = first_cot.astype(jnp.bfloat16)
    gin_ref[...] += dot_nt(first_low, inputs)
    gmid_ref[...] += dot_nt(second_low, first_act)
    gout_ref[...] += dot_nt(second_act, cot_low)

    def lanes(values):
        return sum(values[:, k * BLOCK : (k + 1) * BLOCK] for k in range(GROUP))

    bin_ref[...] += lanes(first_cot)
    bmid_ref[...] += lanes(second_cot)
    bout_ref[...] += lanes(stress_cot)


def greet_lines(me_x, me_y, size_x, size_y):
    barrier = pltpu.get_barrier_semaphore()
    for d in range(1, size_y):
        pl.semaphore_signal(
            barrier,
            inc=1,
            device_id=(me_x, lax.rem(me_y + d, size_y)),
            device_id_type=pl.DeviceIdType.MESH,
        )
    for d in range(1, size_x):
        pl.semaphore_signal(
            barrier,
            inc=1,
            device_id=(lax.rem(me_x + d, size_x), me_y),
            device_id_type=pl.DeviceIdType.MESH,
        )
    pl.semaphore_wait(barrier, size_x + size_y - 2)


def remote(source, target, send, recv, device):
    return pltpu.make_async_remote_copy(
        src_ref=source,
        dst_ref=target,
        send_sem=send,
        recv_sem=recv,
        device_id=device,
        device_id_type=pl.DeviceIdType.MESH,
    )


def line_sum(slots, send, recv, me, size, target):
    copies = []
    for d in range(1, size):
        copy = remote(
            slots.at[me], slots.at[me], send.at[d], recv.at[me], target(lax.rem(me + d, size))
        )
        copy.start()
        copies.append(copy)
    for d in range(1, size):
        other = lax.rem(me + d, size)
        remote(
            slots.at[other], slots.at[other], send.at[d], recv.at[other], target(other)
        ).wait_recv()
    for copy in copies:
        copy.wait_send()
    total = slots[0]
    for k in range(1, size):
        total = total + slots[k]
    return total


def mesh_sum(values, y_slots, x_slots, y_send, y_recv, x_send, x_recv):
    me_x, me_y = lax.axis_index("gx"), lax.axis_index("gy")
    y_slots[me_y] = values
    x_slots[me_x] = line_sum(
        y_slots, y_send, y_recv, me_y, y_slots.shape[0], lambda other: (me_x, other)
    )
    return line_sum(x_slots, x_send, x_recv, me_x, x_slots.shape[0], lambda other: (other, me_y))


def sum_scratch(shape):
    size_x, size_y = lax.axis_size("gx"), lax.axis_size("gy")
    return [
        pltpu.VMEM((size_y,) + shape, jnp.float32),
        pltpu.VMEM((size_x,) + shape, jnp.float32),
        pltpu.SemaphoreType.DMA((size_y,)),
        pltpu.SemaphoreType.DMA((size_y,)),
        pltpu.SemaphoreType.DMA((size_x,)),
        pltpu.SemaphoreType.DMA((size_x,)),
    ]


def grads_kernel(gin_ref, gmid_ref, gout_ref, bin_ref, bmid_ref, bout_ref, out_ref, *slots):
    size_x, size_y = slots[1].shape[0], slots[0].shape[0]
    greet_lines(lax.axis_index("gx"), lax.axis_index("gy"), size_x, size_y)
    hidden = gin_ref.shape[0]
    bout = jnp.sum(bout_ref[...], axis=1, keepdims=True)
    parts = [
        gin_ref[...],
        jnp.sum(bin_ref[...], axis=1, keepdims=True),
        gmid_ref[...],
        jnp.sum(bmid_ref[...], axis=1, keepdims=True),
        gout_ref[...],
        jnp.concatenate([bout, jnp.zeros((hidden - ROWS, 1), jnp.float32)], axis=0),
    ]
    gap = out_ref.shape[1] - sum(part.shape[1] for part in parts)
    joined = jnp.concatenate(parts + [jnp.zeros((hidden, gap), jnp.float32)], axis=1)
    out_ref[...] = mesh_sum(joined, *slots)


def halo_kernel(
    sums_ref, wide_ref, energy_ref, x_halo, y_halo, halo_send, halo_recv, *slots
):
    size_x, size_y = slots[1].shape[0], slots[0].shape[0]
    me_x, me_y = lax.axis_index("gx"), lax.axis_index("gy")
    greet_lines(me_x, me_y, size_x, size_y)
    next_x, last_x = lax.rem(me_x + 1, size_x), lax.rem(me_x + size_x - 1, size_x)
    next_y, last_y = lax.rem(me_y + 1, size_y), lax.rem(me_y + size_y - 1, size_y)
    ends = CX + 2
    copies = [
        remote(
            sums_ref.at[pl.ds(ends - 3, 3)],
            x_halo.at[0],
            halo_send.at[0],
            halo_recv.at[0],
            (next_x, me_y),
        ),
        remote(
            sums_ref.at[pl.ds(0, 3)], x_halo.at[1], halo_send.at[1], halo_recv.at[1], (last_x, me_y)
        ),
    ]
    for copy in copies:
        copy.start()
    inner_y = pl.ds(1, CY + 2)

    def move(x, carry):
        wide_ref[x + 1, inner_y] = sums_ref[x]
        return carry

    lax.fori_loop(2, ends - 2, move, 0)
    for copy in copies:
        copy.wait()
    wide_ref[0, inner_y] = x_halo[0, 0]
    wide_ref[1, inner_y] = sums_ref[0] + x_halo[0, 1]
    wide_ref[2, inner_y] = sums_ref[1] + x_halo[0, 2]
    wide_ref[ends - 1, inner_y] = sums_ref[ends - 2] + x_halo[1, 0]
    wide_ref[ends, inner_y] = sums_ref[ends - 1] + x_halo[1, 1]
    wide_ref[ends + 1, inner_y] = x_halo[1, 2]
    edge = CY + 2
    copies = [
        remote(
            wide_ref.at[:, pl.ds(edge - 2, 3)],
            y_halo.at[0],
            halo_send.at[2],
            halo_recv.at[2],
            (me_x, next_y),
        ),
        remote(
            wide_ref.at[:, pl.ds(1, 3)], y_halo.at[1], halo_send.at[3], halo_recv.at[3], (me_x, last_y)
        ),
    ]
    for copy in copies:
        copy.start()
    for copy in copies:
        copy.wait()

    def fold(x, carry):
        wide_ref[x, 0] = y_halo[0, x, 0]
        wide_ref[x, 1] = wide_ref[x, 1] + y_halo[0, x, 1]
        wide_ref[x, 2] = wide_ref[x, 2] + y_halo[0, x, 2]
        wide_ref[x, edge - 1] = wide_ref[x, edge - 1] + y_halo[1, x, 0]
        wide_ref[x, edge] = wide_ref[x, edge] + y_halo[1, x, 1]
        wide_ref[x, edge + 1] = y_halo[1, x, 2]
        return carry

    lax.fori_loop(0, CX + 4, fold, 0)
    speeds = lax.broadcasted_iota(jnp.int32, (8, NZ), 0) < 3

    def energy_row(x, total):
        cells = wide_ref[x, 2 : CY + 2, 0:8]
        drift = cells * (1.0 / (cells[:, 3:4] + 1.0))
        return total + jnp.sum(drift * drift, axis=0)

    energy = lax.fori_loop(2, CX + 2, energy_row, jnp.zeros((8, NZ), jnp.float32))
    energy_ref[...] = mesh_sum(jnp.where(speeds, energy, 0.0), *slots)


def shards(
    net_inputs,
    velocity,
    particle_mass,
    block_column,
    cell_height,
    block_counts,
    cotangent,
    input_weight,
    input_bias,
    middle_weight,
    middle_bias,
    output_weight,
    output_bias,
):
    tiles_x, tiles_y = lax.axis_size("gx"), lax.axis_size("gy")
    index_x, index_y = lax.axis_index("gx"), lax.axis_index("gy")
    width_x, width_y = CX * tiles_x, CY * tiles_y
    hidden, rows_in = input_weight.shape
    live = lax.dynamic_slice_in_dim(block_counts, index_x * tiles_y + index_y, 1, 0)
    local_x = (block_column // width_y - index_x * CX + 1) % width_x
    local_y = (block_column % width_y - index_y * CY + 1) % width_y
    block_ext = local_x * (CY + 2) + local_y
    mass = particle_mass.reshape(PB, BLOCK)
    height = cell_height.reshape(PB, BLOCK)
    b1 = input_bias[:, None]
    b2 = middle_bias[:, None]
    turned = output_weight.reshape(3, 3, hidden).transpose(1, 0, 2).reshape(9, hidden)
    w3 = jnp.pad(turned, ((4, 3), (0, 0)))
    b3 = jnp.concatenate(
        [jnp.zeros((3,)), jnp.ones((1,)), output_bias.reshape(3, 3).T.reshape(9), jnp.zeros((3,))]
    ).astype(jnp.float32)[:, None]

    def whole(shape):
        return pl.BlockSpec(shape, lambda i, *_: (0,) * len(shape))

    def spread(rows):
        return pl.BlockSpec((rows, SPAN), lambda i, *_: (0, i))

    per_block = pl.BlockSpec((GROUP, BLOCK), lambda i, *_: (i, 0))
    params = pltpu.CompilerParams(vmem_limit_bytes=40 * 1024 * 1024)
    cells = (CX + 2) * (CY + 2)
    sums = pl.pallas_call(
        deposit_kernel,
        out_shape=jax.ShapeDtypeStruct((cells, ROWS, NZ), jnp.float32),
        grid_spec=pltpu.PrefetchScalarGridSpec(
            num_scalar_prefetch=2,
            grid=(PB // GROUP,),
            in_specs=[
                spread(rows_in),
                spread(3),
                per_block,
                per_block,
                spread(3),
                whole((hidden, rows_in)),
                whole((hidden, 1)),
                whole((hidden, hidden)),
                whole((hidden, 1)),
                whole((ROWS, hidden)),
                whole((ROWS, 1)),
            ],
            out_specs=whole((cells, ROWS, NZ)),
        ),
        compiler_params=params,
    )(
        block_ext,
        live,
        net_inputs,
        velocity,
        mass,
        height,
        cotangent,
        input_weight,
        b1,
        middle_weight,
        b2,
        w3,
        b3,
    )
    remote_params = pltpu.CompilerParams(
        collective_id=0, has_side_effects=True, vmem_limit_bytes=40 * 1024 * 1024
    )
    in_vmem = pl.BlockSpec(memory_space=pltpu.VMEM)
    wide_shape = (CX + 4, CY + 4, ROWS, NZ)
    wide, energy_tile = pl.pallas_call(
        halo_kernel,
        out_shape=(
            jax.ShapeDtypeStruct(wide_shape, jnp.float32),
            jax.ShapeDtypeStruct((8, NZ), jnp.float32),
        ),
        in_specs=[in_vmem],
        out_specs=(in_vmem, in_vmem),
        scratch_shapes=[
            pltpu.VMEM((2, 3, CY + 2, ROWS, NZ), jnp.float32),
            pltpu.VMEM((2, CX + 4, 3, ROWS, NZ), jnp.float32),
            pltpu.SemaphoreType.DMA((4,)),
            pltpu.SemaphoreType.DMA((4,)),
        ]
        + sum_scratch((8, NZ)),
        compiler_params=remote_params,
    )(sums.reshape(CX + 2, CY + 2, ROWS, NZ))
    energy = jnp.sum(energy_tile) / (width_x * width_y * NZ)
    step_size = time_scale / jnp.sqrt(energy + epsilon)

    f32 = jnp.float32
    new_velocity, gin, gmid, gout, bin_, bmid, bout = pl.pallas_call(
        gather_kernel,
        out_shape=(
            jax.ShapeDtypeStruct(velocity.shape, f32),
            jax.ShapeDtypeStruct((hidden, rows_in), f32),
            jax.ShapeDtypeStruct((hidden, hidden), f32),
            jax.ShapeDtypeStruct((hidden, ROWS), f32),
            jax.ShapeDtypeStruct((hidden, BLOCK), f32),
            jax.ShapeDtypeStruct((hidden, BLOCK), f32),
            jax.ShapeDtypeStruct((ROWS, BLOCK), f32),
        ),
        grid_spec=pltpu.PrefetchScalarGridSpec(
            num_scalar_prefetch=3,
            grid=(PB // GROUP,),
            in_specs=[
                spread(rows_in),
                per_block,
                per_block,
                whole(wide_shape),
                whole((hidden, rows_in)),
                whole((hidden, 1)),
                whole((hidden, hidden)),
                whole((hidden, 1)),
                whole((hidden, ROWS)),
                whole((hidden, hidden)),
            ],
            out_specs=(
                spread(3),
                whole((hidden, rows_in)),
                whole((hidden, hidden)),
                whole((hidden, ROWS)),
                whole((hidden, BLOCK)),
                whole((hidden, BLOCK)),
                whole((ROWS, BLOCK)),
            ),
            scratch_shapes=[
                pltpu.VMEM(wide_shape, f32),
                pltpu.VMEM((cells, ROWS, NZ), f32),
            ],
        ),
        compiler_params=params,
    )(
        block_ext,
        live,
        step_size.reshape(1),
        net_inputs,
        mass,
        height,
        wide,
        input_weight,
        b1,
        middle_weight,
        b2,
        w3.T,
        middle_weight.T,
    )
    live_total = jnp.sum(block_counts).astype(jnp.float32) * BLOCK
    scale = 1.0 / jnp.sqrt(live_total)
    joined_shape = (hidden, BLOCK)
    assert rows_in + hidden + ROWS + 3 <= BLOCK
    summed = pl.pallas_call(
        grads_kernel,
        out_shape=jax.ShapeDtypeStruct(joined_shape, f32),
        in_specs=[in_vmem] * 6,
        out_specs=in_vmem,
        scratch_shapes=sum_scratch(joined_shape),
        compiler_params=pltpu.CompilerParams(collective_id=1, has_side_effects=True),
    )(gin, gmid, gout, bin_, bmid, bout)
    summed = summed * scale
    mid = rows_in + 1
    out = mid + hidden + 1
    return (
        new_velocity,
        summed[:, 0:rows_in],
        summed[:, rows_in],
        summed[:, mid : mid + hidden],
        summed[:, mid + hidden],
        summed[:, out + 4 : out + 13].reshape(hidden, 3, 3).transpose(2, 1, 0).reshape(9, hidden),
        summed[4:13, out + ROWS].reshape(3, 3).T.reshape(9),
    )


def solution(mesh):
    return jax.shard_map(
        shards,
        mesh=mesh,
        in_specs=(
            P(None, ("gx", "gy")),
            P(None, ("gx", "gy")),
            P(("gx", "gy")),
            P(("gx", "gy")),
            P(("gx", "gy")),
            P(),
            P(None, ("gx", "gy")),
            P(),
            P(),
            P(),
            P(),
            P(),
            P(),
        ),
        out_specs=(P(None, ("gx", "gy")), P(), P(), P(), P(), P(), P()),
        check_vma=False,
    )
```

time: 463 us -> 161 us (0.35); the launches traced: 457 us -> 160 us
  matrix products: 193 us -> 0 us
  Pallas kernels: 0 us -> 120 us
  blocking collectives: 79.2 us -> 0 us
  other arithmetic: 61.4 us -> 2.8 us
  starting transfers between devices: 25.9 us -> 0 us
  waiting for transfers between devices: 22.2 us -> 0 us
  loops' own time: 20.5 us -> 0 us
  local copies, waits for them, and re-layouts: 52.5 us -> 34.7 us
    dot_general x72 -> x0, matrix products: 193 us -> none  [the longest x12 56.1 us: group_read(): jnp.einsum('cbz,bpz->cbp', column_rows, selector, precision=lax.Precision...]
    pallas_call x0 -> x4, Pallas kernels: none -> 120 us  [the longest x1 46.5 us: shards(): pl.pallas_call(halo_kernel, out_shape=(jax.ShapeDtypeStruct(wide_shape, j...]
    psum x2 -> x0, blocking collectives: 79.2 us -> none  [the longest x1 40.5 us: shards(): lax.psum((grad_first_w, grad_first_b, grad_mid_w, grad_mid_b, grad_out_w,...]
    scatter-add x5 -> x0, other arithmetic: 30.6 us -> none  [the longest x1 30.5 us: fold_deposit(): jnp.zeros(((CX + 2) * (CY + 2), channels, NZ), jnp.float32).at[block_ext]]
    ppermute x20 -> x0, starting transfers between devices: 25.9 us -> none  [the longest x10 17.3 us: with_halo(): before = lax.ppermute(last, axis, up)]
    ppermute x20 -> x0, waiting for transfers between devices: 22.2 us -> none  [the longest x10 13.8 us: with_halo(): after = lax.ppermute(initial, axis, down)]
    unnamed x37 -> x60, local copies, waits for them, and re-layouts: 3.35 us -> 24.3 us
    another operation x5 -> x0, loops' own time: 20.5 us -> none  [the longest x2 15.9 us: read_cells(): stacked = lax.map(group_read, jnp.arange(PB // GROUP, dtype=jnp.int32))]
  transfers between devices with their start and end apart: 20 -> 0, of which waited for: 9 -> 0; matrix products, arithmetic and copies ran while one was open for 10% -> 0% of each run, Pallas kernels for 0% -> 0%
where the time goes in v1:
time: 161 us; the launch traced here: 160 us
  Pallas kernels  120 us (75%)
  local copies, waits for them, and re-layouts  34.7 us (22%)
  other arithmetic  2.8 us (2%)
  between operations  2.15 us (1%)
    pallas_call x1, Pallas kernels, shards(): pl.pallas_call(halo_kernel, out_shape=(jax.ShapeDtypeStruct(wide_shape, j...  46.5 us
    pallas_call x1, Pallas kernels, shards(): pl.pallas_call(gather_kernel, out_shape=(jax.ShapeDtypeStruct(velocity.sh...  35.9 us
    unnamed x60, local copies, waits for them, and re-layouts  24.3 us
    pallas_call x1, Pallas kernels, shards(): pl.pallas_call(deposit_kernel, out_shape=jax.ShapeDtypeStruct((cells, ROW...  23.3 us
    pallas_call x1, Pallas kernels, shards(): pl.pallas_call(grads_kernel, out_shape=jax.ShapeDtypeStruct(joined_shape,...  14.4 us

profile of v1, /device:TPU:1, one launch (start us, length us, event | category | flops | bytes accessed | tf_op | source)
XLA Modules:
  0.0 159.7 jit_solution(3644731974473508913)
XLA Ops:
  0.6 1.2 dynamic_slice.3.live_ref
  1.9 0.7 fusion.4.column_ref
  2.6 1.4 copy.53.b1_ref
  3.9 1.4 copy.54.b2_ref
  5.3 0.7 reshape.49
  6.0 0.1 copy.50
  6.3 1.4 copy.52.w1_ref
  7.7 0.7 reshape.51
  8.4 0.1 copy.51
  8.8 1.9 %copy-done = bf16[25,49152]{1,0:T(8,128)(2,1)S(1)} copy-done((bf16[25,49152]{1,0:T(8,128)(2,1)S(1)}, bf16[25,49152]{1,0:T(8,128)(2,1)}, u32[]{:S(2)}) %copy-start) | copy-done | bytes 2457624
  10.6 1.1 copy-done.4
  11.8 1.1 copy-done.5
  12.9 0.9 copy-done.6
  13.8 0.9 copy-done.8
  14.8 0.8 copy-done.10
  15.5 0.8 copy-done.12
  16.3 0.7 copy-done.14
  17.1 0.7 copy-done.16
  17.8 23.3 %shard_map.180 = f32[324,16,128]{2,1,0:T(8,128)S(1)} custom-call(s32[384]{0:T(512)S(1)} %fusion.4.column_ref, s32[1]{0:T(128)} %dynamic_slice.3.live_ref, bf16[25,49152]{1,0:T(8,128)(2,1)S(1)} %copy-done, f32[3,49152]{1,0:T(4,128)S(1)} %copy-done.4, f32[384,128]{1,0:T(8,128)S(1)} %bitcast.21, s32[384,128]{1,0:T(8,128)S(1)} %bitcast.23, ...), custom_call_target="tpu_custom_call" | custom-call | tf_op jit(solution)/shard_map/pallas_call | solution.py:402
  41.1 46.5 %shard_map.181 = (f32[20,20,16,128]{3,2,1,0:T(8,128)S(1)}, f32[8,128]{1,0:T(8,128)S(1)}) custom-call(f32[18,18,16,128]{3,2,1,0:T(8,128)S(1)} %bitcast.20), custom_call_target="tpu_custom_call" | custom-call | tf_op jit(solution)/shard_map/pallas_call | solution.py:444
  87.6 1.7 %copy-done.2 = f32[20,20,16,128]{3,2,1,0:T(8,128)} copy-done((f32[20,20,16,128]{3,2,1,0:T(8,128)}, f32[20,20,16,128]{3,2,1,0:T(8,128)S(1)}, u32[]{:S(2)}) %copy-start.2) | copy-done | bytes 3276824
  89.3 0.6 reduce_sum.18
  90.6 1.4 pad_bitcast_fusion.w3t_ref
  92.0 1.4 copy.57
  93.4 1.9 %copy-done.3 = f32[20,20,16,128]{3,2,1,0:T(8,128)S(1)} copy-done((f32[20,20,16,128]{3,2,1,0:T(8,128)S(1)}, f32[20,20,16,128]{3,2,1,0:T(8,128)}, u32[]{:S(2)}) %copy-start.3) | copy-done | bytes 3276824
  95.3 0.8 copy-done.11
  96.1 0.8 copy-done.13
  96.9 0.7 copy-done.15
  97.6 0.7 copy-done.17
  98.3 0.7 copy-done.18
  99.1 0.7 copy-done.19
  99.8 35.9 %shard_map.182 = (f32[3,49152]{1,0:T(4,128)}, f32[80,25]{1,0:T(8,128)S(1)}, f32[80,80]{1,0:T(8,128)S(1)}, f32[80,16]{1,0:T(8,128)S(1)}, f32[80,128]{1,0:T(8,128)...) custom-call(s32[384]{0:T(512)S(1)} %fusion.4.column_ref, s32[1]{0:T(128)} %dynamic_slice.3.live_ref, ...), custom_call_target="tpu_custom_call" | custom-call | tf_op jit(solution)/shard_map/pallas_call | solution.py:465
  135.7 0.6 copy-done.20
  136.3 0.6 copy-done.21
  136.9 0.6 copy-done.22
  137.5 0.6 copy-done.23
  138.1 0.6 copy-done.24
  138.7 0.6 copy-done.25
  139.3 14.4 %shard_map.183 = f32[80,128]{1,0:T(8,128)} custom-call(f32[80,25]{1,0:T(8,128)} %copy-done.20, f32[80,80]{1,0:T(8,128)} %copy-done.21, f32[80,16]{1,0:T(8,128)} %copy-done.22, f32[80,128]{1,0:T(8,128)} %copy-done.23, f32[80,128]{1,0:T(8,128)} %copy-done.24, f32[16,128]{1,0:T(8,128)} %copy-done.25), custom_call_target="tpu_custom_call" | custom-call | tf_op jit(solution)/shard_map/pallas_call | solution.py:525
  153.8 0.6 reduce_sum.19
  155.1 0.8 broadcast_multiply_fusion
  156.1 0.6 reshape.56
  156.7 0.7 slice.26
  157.4 0.7 copy.64
  158.1 0.2 slice_reduce_fusion.2
  158.3 0.1 copy.63
  158.4 0.6 reshape.57
  159.0 0.7 slice_reduce_fusion
  (46 shorter events, 0.7 us)
Async XLA Ops:
  6.2 2.5 %copy-start.26 = (bf16[9,80]{0,1:T(8,128)(2,1)}, bf16[9,80]{0,1:T(8,128)(2,1)S(1)}, u32[]{:S(2)}) copy-start(bf16[9,80]{0,1:T(8,128)(2,1)S(1)} %copy.50) | copy-start | bytes 4324
  8.8 1.9 %copy-start = (bf16[25,49152]{1,0:T(8,128)(2,1)S(1)}, bf16[25,49152]{1,0:T(8,128)(2,1)}, u32[]{:S(2)}) copy-start(bf16[25,49152]{1,0:T(8,128)(2,1)} %inputs_ref.3) | copy-start | bytes 7372804
  10.6 1.1 copy-start.4
  11.8 1.1 copy-start.5
  12.9 0.9 copy-start.6
  13.8 0.9 copy-start.8
  14.8 0.8 copy-start.10
  15.5 0.8 copy-start.12
  16.3 0.7 copy-start.14
  17.1 0.7 copy-start.16
  17.8 75.6 %copy-start.1 = (bf16[25,49152]{1,0:T(8,128)(2,1)S(1)}, bf16[25,49152]{1,0:T(8,128)(2,1)}, u32[]{:S(2)}) copy-start(bf16[25,49152]{1,0:T(8,128)(2,1)} %inputs_ref.3) | copy-start | bytes 7372804
  17.8 75.6 %copy-start.7 = (f32[49152]{0:T(1024)S(1)}, f32[49152]{0:T(1024)}, u32[]{:S(2)}) copy-start(f32[49152]{0:T(1024)} %param.15) | copy-start | bytes 589828
  17.8 75.6 %copy-start.9 = (s32[49152]{0:T(1024)S(1)}, s32[49152]{0:T(1024)}, u32[]{:S(2)}) copy-start(s32[49152]{0:T(1024)} %param.17) | copy-start | bytes 589828
  87.6 1.7 %copy-start.2 = (f32[20,20,16,128]{3,2,1,0:T(8,128)}, f32[20,20,16,128]{3,2,1,0:T(8,128)S(1)}, u32[]{:S(2)}) copy-start(f32[20,20,16,128]{3,2,1,0:T(8,128)S(1)} %get-tuple-element.17.wide_ref) | copy-start | bytes 9830404
  93.4 1.9 %copy-start.3 = (f32[20,20,16,128]{3,2,1,0:T(8,128)S(1)}, f32[20,20,16,128]{3,2,1,0:T(8,128)}, u32[]{:S(2)}) copy-start(f32[20,20,16,128]{3,2,1,0:T(8,128)} %copy-done.2) | copy-start | bytes 9830404
  95.3 0.8 copy-start.11
  96.1 0.8 copy-start.13
  96.9 0.7 copy-start.15
  97.6 0.7 copy-start.17
  98.3 0.7 copy-start.18
  99.1 0.7 copy-start.19
  99.8 54.0 %copy-start.27 = (s32[32]{0:T(128)S(1)}, s32[32]{0:T(128)}, u32[]{:S(2)}) copy-start(s32[32]{0:T(128)} %param.18) | copy-start | bytes 388
  135.7 0.6 copy-start.20
  136.3 0.6 copy-start.21
  136.9 0.6 copy-start.22
  137.5 0.6 copy-start.23
  138.1 0.6 copy-start.24
  138.7 0.6 copy-start.25

commit v2 on v1

--- a/solution.py
+++ b/solution.py
@@ -301,7 +301,25 @@
             sums_ref.at[pl.ds(0, 3)], x_halo.at[1], halo_send.at[1], halo_recv.at[1], (last_x, me_y)
         ),
     ]
-    for copy in copies:
+    edge = CY + 2
+    still, still_wide = pl.ds(2, CX - 2), pl.ds(3, CX - 2)
+    early = [
+        remote(
+            sums_ref.at[still, pl.ds(edge - 3, 3)],
+            y_halo.at[0, still_wide],
+            halo_send.at[2],
+            halo_recv.at[2],
+            (me_x, next_y),
+        ),
+        remote(
+            sums_ref.at[still, pl.ds(0, 3)],
+            y_halo.at[1, still_wide],
+            halo_send.at[3],
+            halo_recv.at[3],
+            (me_x, last_y),
+        ),
+    ]
+    for copy in copies + early:
         copy.start()
     inner_y = pl.ds(1, CY + 2)
 
@@ -318,22 +336,22 @@
     wide_ref[ends - 1, inner_y] = sums_ref[ends - 2] + x_halo[1, 0]
     wide_ref[ends, inner_y] = sums_ref[ends - 1] + x_halo[1, 1]
     wide_ref[ends + 1, inner_y] = x_halo[1, 2]
-    edge = CY + 2
-    copies = [
-        remote(
-            wide_ref.at[:, pl.ds(edge - 2, 3)],
-            y_halo.at[0],
-            halo_send.at[2],
-            halo_recv.at[2],
-            (me_x, next_y),
-        ),
-        remote(
-            wide_ref.at[:, pl.ds(1, 3)], y_halo.at[1], halo_send.at[3], halo_recv.at[3], (me_x, last_y)
-        ),
-    ]
+    copies = []
+    for k, rows in enumerate((pl.ds(0, 3), pl.ds(CX + 1, 3))):
+        for side, start, device in ((0, edge - 2, next_y), (1, 1, last_y)):
+            number = 4 + 2 * k + side
+            copies.append(
+                remote(
+                    wide_ref.at[rows, pl.ds(start, 3)],
+                    y_halo.at[side, rows],
+                    halo_send.at[number],
+                    halo_recv.at[number],
+                    (me_x, device),
+                )
+            )
     for copy in copies:
         copy.start()
-    for copy in copies:
+    for copy in early + copies:
         copy.wait()
 
     def fold(x, carry):
@@ -452,8 +470,8 @@
         scratch_shapes=[
             pltpu.VMEM((2, 3, CY + 2, ROWS, NZ), jnp.float32),
             pltpu.VMEM((2, CX + 4, 3, ROWS, NZ), jnp.float32),
-            pltpu.SemaphoreType.DMA((4,)),
-            pltpu.SemaphoreType.DMA((4,)),
+            pltpu.SemaphoreType.DMA((8,)),
+            pltpu.SemaphoreType.DMA((8,)),
         ]
         + sum_scratch((8, NZ)),
         compiler_params=remote_params,

time: 161 us -> 151 us (0.938)
  Pallas kernels: 120 us -> 110 us
    pallas_call x1, Pallas kernels: 46.5 us -> 35.8 us  [shards(): pl.pallas_call(halo_kernel, out_shape=(jax.ShapeDtypeStruct(wide_shape, j...]
where the time goes in v2:
time: 151 us; the launch traced here: 150 us
  Pallas kernels  110 us (73%)
  local copies, waits for them, and re-layouts  34.7 us (23%)
  other arithmetic  2.8 us (2%)
  between operations  2.15 us (1%)
    pallas_call x1, Pallas kernels, shards(): pl.pallas_call(gather_kernel, out_shape=(jax.ShapeDtypeStruct(velocity.sh...  35.9 us
    pallas_call x1, Pallas kernels, shards(): pl.pallas_call(halo_kernel, out_shape=(jax.ShapeDtypeStruct(wide_shape, j...  35.8 us
    unnamed x60, local copies, waits for them, and re-layouts  24.3 us
    pallas_call x1, Pallas kernels, shards(): pl.pallas_call(deposit_kernel, out_shape=jax.ShapeDtypeStruct((cells, ROW...  23.3 us
    pallas_call x1, Pallas kernels, shards(): pl.pallas_call(grads_kernel, out_shape=jax.ShapeDtypeStruct(joined_shape,...  15.2 us

profile of v2, /device:TPU:1, one launch (start us, length us, event | category | flops | bytes accessed | tf_op | source)
XLA Modules:
  0.0 149.8 jit_solution(5930860740238948063)
XLA Ops:
  0.6 1.2 dynamic_slice.3.live_ref
  1.9 0.7 fusion.4.column_ref
  2.6 1.4 copy.53.b1_ref
  3.9 1.4 copy.54.b2_ref
  5.3 0.7 reshape.49
  6.0 0.1 copy.50
  6.3 1.4 copy.52.w1_ref
  7.7 0.7 reshape.51
  8.4 0.1 copy.51
  8.8 1.9 %copy-done = bf16[25,49152]{1,0:T(8,128)(2,1)S(1)} copy-done((bf16[25,49152]{1,0:T(8,128)(2,1)S(1)}, bf16[25,49152]{1,0:T(8,128)(2,1)}, u32[]{:S(2)}) %copy-start) | copy-done | bytes 2457624
  10.6 1.1 copy-done.4
  11.8 1.1 copy-done.5
  12.9 0.9 copy-done.6
  13.8 0.9 copy-done.8
  14.8 0.8 copy-done.10
  15.5 0.8 copy-done.12
  16.3 0.7 copy-done.14
  17.1 0.7 copy-done.16
  17.8 23.3 %shard_map.180 = f32[324,16,128]{2,1,0:T(8,128)S(1)} custom-call(s32[384]{0:T(512)S(1)} %fusion.4.column_ref, s32[1]{0:T(128)} %dynamic_slice.3.live_ref, bf16[25,49152]{1,0:T(8,128)(2,1)S(1)} %copy-done, f32[3,49152]{1,0:T(4,128)S(1)} %copy-done.4, f32[384,128]{1,0:T(8,128)S(1)} %bitcast.21, s32[384,128]{1,0:T(8,128)S(1)} %bitcast.23, ...), custom_call_target="tpu_custom_call" | custom-call | tf_op jit(solution)/shard_map/pallas_call | solution.py:420
  41.1 35.8 %shard_map.181 = (f32[20,20,16,128]{3,2,1,0:T(8,128)S(1)}, f32[8,128]{1,0:T(8,128)S(1)}) custom-call(f32[18,18,16,128]{3,2,1,0:T(8,128)S(1)} %bitcast.20), custom_call_target="tpu_custom_call" | custom-call | tf_op jit(solution)/shard_map/pallas_call | solution.py:462
  76.9 1.7 %copy-done.2 = f32[20,20,16,128]{3,2,1,0:T(8,128)} copy-done((f32[20,20,16,128]{3,2,1,0:T(8,128)}, f32[20,20,16,128]{3,2,1,0:T(8,128)S(1)}, u32[]{:S(2)}) %copy-start.2) | copy-done | bytes 3276824
  78.5 0.6 reduce_sum.18
  79.8 1.4 pad_bitcast_fusion.w3t_ref
  81.2 1.4 copy.57
  82.7 1.9 %copy-done.3 = f32[20,20,16,128]{3,2,1,0:T(8,128)S(1)} copy-done((f32[20,20,16,128]{3,2,1,0:T(8,128)S(1)}, f32[20,20,16,128]{3,2,1,0:T(8,128)}, u32[]{:S(2)}) %copy-start.3) | copy-done | bytes 3276824
  84.6 0.8 copy-done.11
  85.4 0.8 copy-done.13
  86.2 0.7 copy-done.15
  86.9 0.7 copy-done.17
  87.6 0.7 copy-done.18
  88.3 0.7 copy-done.19
  89.1 35.9 %shard_map.182 = (f32[3,49152]{1,0:T(4,128)}, f32[80,25]{1,0:T(8,128)S(1)}, f32[80,80]{1,0:T(8,128)S(1)}, f32[80,16]{1,0:T(8,128)S(1)}, f32[80,128]{1,0:T(8,128)...) custom-call(s32[384]{0:T(512)S(1)} %fusion.4.column_ref, s32[1]{0:T(128)} %dynamic_slice.3.live_ref, ...), custom_call_target="tpu_custom_call" | custom-call | tf_op jit(solution)/shard_map/pallas_call | solution.py:483
  124.9 0.6 copy-done.20
  125.5 0.6 copy-done.21
  126.2 0.6 copy-done.22
  126.8 0.6 copy-done.23
  127.4 0.6 copy-done.24
  128.0 0.6 copy-done.25
  128.6 15.2 %shard_map.183 = f32[80,128]{1,0:T(8,128)} custom-call(f32[80,25]{1,0:T(8,128)} %copy-done.20, f32[80,80]{1,0:T(8,128)} %copy-done.21, f32[80,16]{1,0:T(8,128)} %copy-done.22, f32[80,128]{1,0:T(8,128)} %copy-done.23, f32[80,128]{1,0:T(8,128)} %copy-done.24, f32[16,128]{1,0:T(8,128)} %copy-done.25), custom_call_target="tpu_custom_call" | custom-call | tf_op jit(solution)/shard_map/pallas_call | solution.py:543
  143.8 0.6 reduce_sum.19
  145.1 0.8 broadcast_multiply_fusion
  146.1 0.6 reshape.56
  146.7 0.7 slice.26
  147.4 0.7 copy.64
  148.1 0.2 slice_reduce_fusion.2
  148.4 0.1 copy.63
  148.5 0.6 reshape.57
  149.1 0.7 slice_reduce_fusion
  (46 shorter events, 0.7 us)
Async XLA Ops:
  6.2 2.5 %copy-start.26 = (bf16[9,80]{0,1:T(8,128)(2,1)}, bf16[9,80]{0,1:T(8,128)(2,1)S(1)}, u32[]{:S(2)}) copy-start(bf16[9,80]{0,1:T(8,128)(2,1)S(1)} %copy.50) | copy-start | bytes 4324
  8.8 1.9 %copy-start = (bf16[25,49152]{1,0:T(8,128)(2,1)S(1)}, bf16[25,49152]{1,0:T(8,128)(2,1)}, u32[]{:S(2)}) copy-start(bf16[25,49152]{1,0:T(8,128)(2,1)} %inputs_ref.3) | copy-start | bytes 7372804
  10.6 1.1 copy-start.4
  11.8 1.1 copy-start.5
  12.9 0.9 copy-start.6
  13.8 0.9 copy-start.8
  14.8 0.8 copy-start.10
  15.5 0.8 copy-start.12
  16.3 0.7 copy-start.14
  17.1 0.7 copy-start.16
  17.8 64.9 %copy-start.1 = (bf16[25,49152]{1,0:T(8,128)(2,1)S(1)}, bf16[25,49152]{1,0:T(8,128)(2,1)}, u32[]{:S(2)}) copy-start(bf16[25,49152]{1,0:T(8,128)(2,1)} %inputs_ref.3) | copy-start | bytes 7372804
  17.8 64.9 %copy-start.7 = (f32[49152]{0:T(1024)S(1)}, f32[49152]{0:T(1024)}, u32[]{:S(2)}) copy-start(f32[49152]{0:T(1024)} %param.15) | copy-start | bytes 589828
  17.8 64.9 %copy-start.9 = (s32[49152]{0:T(1024)S(1)}, s32[49152]{0:T(1024)}, u32[]{:S(2)}) copy-start(s32[49152]{0:T(1024)} %param.17) | copy-start | bytes 589828
  76.9 1.7 %copy-start.2 = (f32[20,20,16,128]{3,2,1,0:T(8,128)}, f32[20,20,16,128]{3,2,1,0:T(8,128)S(1)}, u32[]{:S(2)}) copy-start(f32[20,20,16,128]{3,2,1,0:T(8,128)S(1)} %get-tuple-element.17.wide_ref) | copy-start | bytes 9830404
  82.7 1.9 %copy-start.3 = (f32[20,20,16,128]{3,2,1,0:T(8,128)S(1)}, f32[20,20,16,128]{3,2,1,0:T(8,128)}, u32[]{:S(2)}) copy-start(f32[20,20,16,128]{3,2,1,0:T(8,128)} %copy-done.2) | copy-start | bytes 9830404
  84.6 0.8 copy-start.11
  85.4 0.8 copy-start.13
  86.2 0.7 copy-start.15
  86.9 0.7 copy-start.17
  87.6 0.7 copy-start.18
  88.3 0.7 copy-start.19
  89.1 54.7 %copy-start.27 = (s32[32]{0:T(128)S(1)}, s32[32]{0:T(128)}, u32[]{:S(2)}) copy-start(s32[32]{0:T(128)} %param.18) | copy-start | bytes 388
  124.9 0.6 copy-start.20
  125.5 0.6 copy-start.21
  126.2 0.6 copy-start.22
  126.8 0.6 copy-start.23
  127.4 0.6 copy-start.24
  128.0 0.6 copy-start.25
